TPU v7x, 256 devices: a whole 4x4x8 slice. The times are simulated.
256 devices in a mesh: feat: 32 (over x, y, z_lo), dp: 8 (over z_hi, core).
Axes of the slice: x: 4, y: 4, z: 8 (z_hi: 4, z_lo: 2; z = z_hi * 2 + z_lo), core: 2. Of those that a mesh axis runs over, the one named last changes fastest.
Arguments:
- activations: bfloat16 [4096, 16384], P('dp', 'feat')
- norm_gain: float32 [16384], replicated, may hold values from 0.5 to 1.5
- weights: float32 [4096, 16384], P('dp', 'feat'), may hold values from -6 to 6
- inverse_factor: float32 [128, 16384], P(None, 'feat'), as said below
- grid_scales: float32 [4096], P('dp'), may hold values from 0.5 to 2
Outputs:
- hessian: float32 [16384, 16384], P('dp', 'feat')
- updated_weights: float32 [4096, 16384], P('dp', 'feat')
Inputs may be any that keep to these rules, and one draw needn't show every extreme that they name: `inverse_factor`: in the first 128 columns, the diagonal lies in 1 to 2 and entries below it are zero.
All inputs are finite; a program needn't handle non-finite values.
Results may differ from a plain program's by a relative error of at most 0.012.
Values may be sent and summed in bfloat16 or wider, within the bound.
A program may use at most 128 MiB of HBM per device.

v0:
```python
import math

import jax
import jax.numpy as jnp
from jax import lax
from jax.sharding import PartitionSpec as P

norm_epsilon = 1e-05
full_turn = 2.0 * math.pi


def spread(value, axis, source):
    kept = jnp.where(lax.axis_index(axis) == source, value, 0).astype(value.dtype)
    return lax.psum(kept, axis)


def quantize_panel(panel_rows, factor_block, grid_scales):
    panel_width = factor_block.shape[0]
    diagonal_entries = jnp.diagonal(factor_block)
    positions = jnp.arange(panel_width)

    def advance(index, carry):
        working, quantized, residue = carry
        current = lax.dynamic_index_in_dim(working, index, 0, keepdims=False)
        grid_ratio = current / grid_scales
        dequantized = grid_scales * (grid_ratio - jnp.sin(full_turn * grid_ratio) / full_turn)
        pivot_entry = lax.dynamic_index_in_dim(diagonal_entries, index, 0, keepdims=False)
        scaled_error = (current - dequantized) / pivot_entry
        factor_row = lax.dynamic_index_in_dim(factor_block, index, 0, keepdims=False)
        factor_row = jnp.where(positions > index, factor_row, jnp.zeros_like(factor_row))
        working = working - factor_row[:, None] * scaled_error[None, :]
        quantized = lax.dynamic_update_index_in_dim(quantized, dequantized, index, 0)
        residue = lax.dynamic_update_index_in_dim(residue, scaled_error, index, 0)
        return (working, quantized, residue)

    blank = jnp.zeros_like(panel_rows)
    final = lax.fori_loop(0, panel_width, advance, (panel_rows, blank, blank))
    return (final[1], final[2])


def body(activations, norm_gain, weights, inverse_factor, grid_scales):
    shard_width = activations.shape[1]
    row_count = activations.shape[0]
    full_width = shard_width * lax.axis_size("feat")
    token_total = row_count * lax.axis_size("dp")
    own_start = lax.axis_index("feat") * shard_width
    own_gain = lax.dynamic_slice_in_dim(norm_gain, own_start, shard_width, 0)
    widened = activations.astype(jnp.float32)
    own_squares = jnp.sum(widened * widened, axis=1, keepdims=True)
    row_squares = lax.psum(own_squares, "feat")
    normed = (
        widened * lax.rsqrt(row_squares / full_width + norm_epsilon) * own_gain[None, :]
    ).astype(jnp.bfloat16)
    gathered = lax.all_gather(normed, "feat", axis=1, tiled=True)
    product = lax.dot_general(
        gathered, normed, (((0,), (0,)), ((), ())), preferred_element_type=jnp.float32
    )
    hessian = lax.psum_scatter(
        (product / token_total).astype(jnp.bfloat16), "dp", scatter_dimension=0, tiled=True
    ).astype(jnp.float32)
    panel_width = inverse_factor.shape[0]
    quantized, residue = quantize_panel(
        weights[:, :panel_width].T, inverse_factor[:, :panel_width], grid_scales
    )
    residue = spread(residue.astype(jnp.bfloat16), "feat", 0).astype(residue.dtype)
    shift_terms = lax.dot_general(
        residue,
        inverse_factor,
        (((0,), (0,)), ((), ())),
        precision=lax.Precision.HIGHEST,
        preferred_element_type=jnp.float32,
    )
    updated = weights - shift_terms
    column_ids = lax.broadcasted_iota(jnp.int32, weights.shape, 1)
    panel_mask = (column_ids < panel_width) & (lax.axis_index("feat") == 0)
    padded_panel = jnp.pad(quantized.T, ((0, 0), (0, shard_width - panel_width)))
    updated = jnp.where(panel_mask, padded_panel, updated)
    return (hessian, updated)


def solution(mesh):
    placed = (P("dp", "feat"), P(), P("dp", "feat"), P(None, "feat"), P("dp"))
    return jax.shard_map(
        body,
        mesh=mesh,
        in_specs=placed,
        out_specs=(P("dp", "feat"), P("dp", "feat")),
        check_vma=False,
    )
```

profile of v0, /device:TPU:60, one launch (start us, length us, event | category | flops | bytes accessed | tf_op | source)
XLA Modules:
  0.0 934.6 jit_solution(16510306235516055651)
XLA Ops:
  8.4 67.3 %psum.14 = f32[512,1]{0,1:T(1,128)S(1)} all-reduce(f32[512,1]{0,1:T(1,128)S(1)} %bitcast.28), channel_id=1, replica_groups=mesh['feat'=32,'dp'=8] {'feat'}, use_global_device_ids=true, to_apply=%region_1.0 | all-reduce | flops 512 | bytes 4096 | tf_op jit(solution)/shard_map/psum | solution.py:50
  76.5 2.0 fusion.5
  81.8 289.4 %while.18 = (s32[]{:T(128)}, f32[128,512]{1,0:T(8,128)S(1)}, f32[128,512]{1,0:T(8,128)S(1)}, bf16[128,512]{1,0:T(8,128)(2,1)S(1)}, f32[128,128]{1,0:T(8,128)S(1)...) while((s32[]{:T(128)}, f32[128,512]{1,0:T(8,128)S(1)}, f32[128,512]{1,0:T(8,128)S(1)}, ...), condition=%wide.region_4.5_spmd.clone, body=%wide.region_3.4_spmd.clone.sunk | while | flops 134914 | bytes 545401 | solution.py:37
  107.3 1.4 subtract_divide_fusion.2
  116.4 1.4 subtract_divide_fusion.2
  118.6 1.4 subtract_divide_fusion.2
  120.9 1.4 subtract_divide_fusion.2
  127.7 1.4 subtract_divide_fusion.2
  130.0 1.4 subtract_divide_fusion.2
  132.2 1.4 subtract_divide_fusion.2
  136.7 1.4 subtract_divide_fusion.2
  139.0 1.4 subtract_divide_fusion.2
  141.3 1.4 subtract_divide_fusion.2
  143.5 1.4 subtract_divide_fusion.2
  154.8 1.4 subtract_divide_fusion.2
  161.6 1.4 subtract_divide_fusion.2
  166.1 1.4 subtract_divide_fusion.2
  172.9 1.4 subtract_divide_fusion.2
  175.2 1.4 subtract_divide_fusion.2
  177.4 1.4 subtract_divide_fusion.2
  182.0 1.4 subtract_divide_fusion.2
  184.2 1.4 subtract_divide_fusion.2
  186.5 1.4 subtract_divide_fusion.2
  188.8 1.4 subtract_divide_fusion.2
  197.8 1.4 subtract_divide_fusion.2
  200.1 1.4 subtract_divide_fusion.2
  206.8 1.4 subtract_divide_fusion.2
  209.1 1.4 subtract_divide_fusion.2
  211.4 1.4 subtract_divide_fusion.2
  213.6 1.4 subtract_divide_fusion.2
  220.4 1.4 subtract_divide_fusion.2
  222.7 1.4 subtract_divide_fusion.2
  224.9 1.4 subtract_divide_fusion.2
  231.7 1.4 subtract_divide_fusion.2
  236.2 1.4 subtract_divide_fusion.2
  243.0 1.4 subtract_divide_fusion.2
  247.5 1.4 subtract_divide_fusion.2
  252.1 1.4 subtract_divide_fusion.2
  254.3 1.4 subtract_divide_fusion.2
  256.6 1.4 subtract_divide_fusion.2
  258.9 1.4 subtract_divide_fusion.2
  265.6 1.4 subtract_divide_fusion.2
  267.9 1.4 subtract_divide_fusion.2
  270.2 1.4 subtract_divide_fusion.2
  276.9 1.4 subtract_divide_fusion.2
  279.2 1.4 subtract_divide_fusion.2
  281.5 1.4 subtract_divide_fusion.2
  290.5 1.4 subtract_divide_fusion.2
  292.8 1.4 subtract_divide_fusion.2
  301.8 1.4 subtract_divide_fusion.2
  304.1 1.4 subtract_divide_fusion.2
  306.3 1.4 subtract_divide_fusion.2
  313.1 1.4 subtract_divide_fusion.2
  315.4 1.4 subtract_divide_fusion.2
  317.6 1.4 subtract_divide_fusion.2
  324.4 1.4 subtract_divide_fusion.2
  326.7 1.4 subtract_divide_fusion.2
  358.4 1.4 subtract_divide_fusion.2
  372.0 81.8 %all-gather.2.cloned.1.call-done = bf16[512,16384]{1,0:T(8,128)(2,1)} async-done(((bf16[512,512]{1,0:T(8,128)(2,1)}), bf16[512,16384]{1,0:T(8,128)(2,1)}) %all-gather.2.cloned.1.call-update) | async-done | bytes 16777232 | tf_op jit(solution)/shard_map/all_gather | solution.py:54
  453.9 15.8 %multiply_convert_fusion = bf16[16384,512]{1,0:T(8,128)(2,1)} fusion(bf16[512,16384]{1,0:T(8,128)(2,1)} %all-gather.2.cloned.1.call-done, bf16[512,512]{1,0:T(8,128)(2,1)} %fusion.5), kind=kOutput, calls=%fused_computation.6 | convolution fusion | flops 8606711808 | bytes 34078720 | tf_op jit(solution)/shard_map/dot_general | solution.py:55
  469.8 261.9 %all-reduce.3.cloned.1.call-done = bf16[128,512]{1,0:T(8,128)(2,1)} async-done(((bf16[128,512]{1,0:T(8,128)(2,1)}), bf16[128,512]{1,0:T(8,128)(2,1)}) %all-reduce.3.cloned.1.call-update) | async-done | bytes 131088 | tf_op jit(solution)/shard_map/psum | solution.py:14
  731.7 2.5 fusion.2
  734.3 189.7 %reduce-scatter.2.cloned.1.call-done = bf16[2048,512]{1,0:T(8,128)(2,1)} async-done(((bf16[16384,512]{1,0:T(8,128)(2,1)}), bf16[2048,512]{1,0:T(8,128)(2,1)}) %reduce-scatter.2.cloned.1.call-update) | async-done | bytes 2097168 | tf_op jit(solution)/shard_map/reduce_scatter | solution.py:58
  923.9 4.2 convert_element_type.23
  (736 shorter events, 214.1 us)
Async XLA Ops:
  7.2 446.7 %all-gather.2.cloned.1.call-start = ((), (), s32[]{:S(2)}) async-start(), calls=%async_computation.1 | async-start | bytes 17301504 | tf_op jit(solution)/shard_map/all_gather | solution.py:54
  78.5 653.2 %all-reduce.3.cloned.1.call-start = ((), (), s32[]{:S(2)}) async-start(), calls=%async_computation.3 | async-start | bytes 262144 | tf_op jit(solution)/shard_map/psum | solution.py:14
  372.0 551.9 %reduce-scatter.2.cloned.1.call-start = ((), (), s32[]{:S(2)}) async-start(), calls=%async_computation.2 | async-start | bytes 18874368 | tf_op jit(solution)/shard_map/reduce_scatter | solution.py:58
  469.7 262.1 %copy-start = (f32[512,512]{1,0:T(8,128)S(1)}, f32[512,512]{1,0:T(8,128)}, u32[]{:S(2)}) copy-start(f32[512,512]{1,0:T(8,128)} %param.9) | copy-start | bytes 3145732
  469.7 262.1 %copy-start.1 = (f32[128,512]{1,0:T(8,128)S(1)}, f32[128,512]{1,0:T(8,128)}, u32[]{:S(2)}) copy-start(f32[128,512]{1,0:T(8,128)} %param.10) | copy-start | bytes 786436
Sparse Core Ops, SparseCore 0:
  78.7 375.1 all-gather.1
  457.1 274.6 all-reduce.2
  734.5 189.3 reduce-scatter.1
where the time goes:
time: 941 us; the launch traced here: 935 us
  waiting for transfers between devices  533 us (57%)
  other arithmetic  199 us (21%)
  local copies, waits for them, and re-layouts  97.2 us (10%)
  blocking collectives  67.3 us (7%)
  matrix products  18.3 us (2%)
  between operations  13.8 us (1%)
    psum x1, waiting for transfers between devices, spread(): return lax.psum(kept, axis)  262 us
    reduce_scatter x1, waiting for transfers between devices, body(): lax.psum_scatter((product / token_total).astype(jnp.bfloat16), 'dp', scat...  190 us
    div x128, other arithmetic, advance(): scaled_error = (current - dequantized) / pivot_entry  176 us
    all_gather x1, waiting for transfers between devices, body(): gathered = lax.all_gather(normed, 'feat', axis=1, tiled=True)  81.8 us
    dynamic_slice x128, local copies, waits for them, and re-layouts, advance(): lax.dynamic_index_in_dim(diagonal_entries, index, 0, keepdims=False)  79.3 us
    psum x1, blocking collectives, body(): row_squares = lax.psum(own_squares, 'feat')  67.3 us
  transfers between devices with their start and end apart: 3, of which 3 were waited for; matrix products, arithmetic and copies ran while one was open for 33% of the time, Pallas kernels for 0%

commit v1 on v0

v1 whole, which is shorter than its diff:
```python
import jax
import jax.numpy as jnp
from jax import lax
from jax.experimental import pallas as pl
from jax.experimental.pallas import tpu as pltpu
from jax.sharding import PartitionSpec as P

norm_epsilon = 1e-05
sine_terms = (
    0.9999999992570509,
    -6.579735975330413,
    12.987860041709927,
    -12.207664043572143,
    6.688634017511125,
    -2.3713842475866285,
    0.5153655900715548,
)
MESH = pl.DeviceIdType.MESH
f32 = jnp.float32
bf16 = jnp.bfloat16


def wave(ratio):
    part = ratio - jnp.round(ratio)
    square = part * part
    total = jnp.full_like(square, sine_terms[-1])
    for term in sine_terms[-2::-1]:
        total = total * square + term
    return part * total


def panel_kernel(weights, factor, grid_scales, quantized, residue, ratios, waves):
    panel = factor.shape[0]
    block = factor[:, :panel]
    rows = lax.broadcasted_iota(jnp.int32, (panel, panel), 0)
    lanes = lax.broadcasted_iota(jnp.int32, (panel, panel), 1)
    diagonal = jnp.sum(jnp.where(rows == lanes, block, 0.0), axis=1, keepdims=True)
    scaled = jnp.where(lanes > rows, block / diagonal, 0.0)
    turned = scaled.T
    scale = grid_scales[...]
    ratios[...] = weights[:, :panel].T / scale
    for base in range(0, panel, 8):
        tile = ratios[base : base + 8, :]
        for step in range(8):
            row = base + step
            current = jnp.broadcast_to(tile[step : step + 1, :], tile.shape)
            bump = wave(current)
            waves[row : row + 1, :] = bump[:1, :]
            quantized[row : row + 1, :] = scale * (current - bump)[:1, :]
            tile = tile - turned[base : base + 8, row : row + 1] * bump
        if base + 8 < panel:
            ratios[base + 8 :, :] -= lax.dot_general(
                scaled[base : base + 8, base + 8 :],
                waves[base : base + 8, :],
                (((0,), (0,)), ((), ())),
                precision=lax.Precision.HIGHEST,
                preferred_element_type=f32,
            )
    residue[...] = (waves[...] * scale / diagonal).astype(bf16)


def push(source, target, sent, got, device):
    return pltpu.make_async_remote_copy(
        src_ref=source,
        dst_ref=target,
        send_sem=sent,
        recv_sem=got,
        device_id=device,
        device_id_type=MESH,
    )


def main_kernel(
    act,
    gain,
    weights,
    factor,
    quantized,
    residue,
    hessian,
    updated,
    raw,
    scaled,
    rows,
    total,
    away,
    home,
    stat_x,
    stat_y,
    stat_z,
    stat_all,
    error,
    own_sem,
    z_sent,
    z_got,
    twin_sent,
    twin_got,
    row_sent,
    row_got,
    sx_sent,
    sx_got,
    sy_sent,
    sy_got,
    sz_sent,
    sz_got,
    st_sent,
    st_got,
    err_sent,
    err_got,
    part_sent,
    part_got,
):
    rem, div = lax.rem, lax.div
    feat = lax.axis_index("feat")
    data = lax.axis_index("dp")
    x, y, zl = div(feat, 8), rem(div(feat, 2), 4), rem(feat, 2)
    zh, core = div(data, 2), rem(data, 2)
    z = zh * 2 + zl
    sign = 1 - 2 * core

    def device(x_, y_, z_, core_):
        return ((x_ * 4 + y_) * 2 + rem(z_, 2), div(z_, 2) * 2 + core_)

    def along(step):
        return rem(z + 8 + step, 8)

    right, left = rem(x + 1, 4), rem(x + 3, 4)
    above, below = rem(y + 1, 4), rem(y + 3, 4)
    twin = device(x, y, z, 1 - core)
    ahead = device(x, y, along(sign), core)
    behind = device(x, y, along(-sign), core)
    partner = device(x, y, zh * 2 + 1 - zl, core)
    sides = (
        device(right, y, z, core),
        device(left, y, z, core),
        device(x, above, z, core),
        device(x, below, z, core),
    )

    barrier = pltpu.get_barrier_semaphore()
    peers = [twin]
    peers += [device(rem(x + k, 4), y, z, core) for k in (1, 2, 3)]
    peers += [device(x, rem(y + k, 4), z, core) for k in (1, 2, 3)]
    peers += [device(x, y, along(k), core) for k in range(1, 8)]
    for peer in peers:
        pl.semaphore_signal(barrier, inc=1, device_id=peer, device_id_type=MESH)
    pl.semaphore_wait(barrier, len(peers))

    def slot(z_, core_):
        return raw.at[rem(z_, 2), div(z_, 2) * 2 + core_]

    def ring(stream, hop, source=None):
        origin = along(-sign * hop if stream == 0 else sign * hop)
        place = slot(origin, core)
        index = hop + 4 * stream
        return push(
            place if source is None else source,
            place,
            z_sent.at[index],
            z_got.at[index],
            ahead if stream == 0 else behind,
        )

    def ring_wait(stream, hop):
        origin = along(-sign * hop if stream == 0 else sign * hop)
        place = slot(origin, core)
        index = hop - 1 + 4 * stream
        push(place, place, z_sent.at[index], z_got.at[index], ahead).wait_recv()

    def share(index, source=None):
        stream, hop = (1, index - 4) if index > 4 else (0, index)
        place = slot(along(-sign * hop if stream == 0 else sign * hop), core)
        return push(
            place if source is None else source,
            place,
            twin_sent.at[index],
            twin_got.at[index],
            twin,
        )

    def share_wait(index):
        stream, hop = (1, index - 4) if index > 4 else (0, index)
        place = slot(along(sign * hop if stream == 0 else -sign * hop), 1 - core)
        push(place, place, twin_sent.at[index], twin_got.at[index], twin).wait_recv()

    offsets = (0, -sign, sign, 2)
    dx = rem(x + 4 - zh, 4)
    dy = [rem(y + 4 - (2 * core + s), 4) for s in (0, 1)]
    hops = [
        jnp.minimum(dx, 4 - dx) + jnp.minimum(dy[s], 4 - dy[s]) for s in (0, 1)
    ]

    def block_index(o):
        part = core if o % 2 == 0 else 1 - core
        return rem(zh + 4 + offsets[o // 2], 4) * 2 + part

    def sends(s, o):
        side_x, side_y = (1, 1) if o % 2 == 0 else (3, 3)
        spread = dy[s] == 0
        out_x = [dx == 0, dx == 0]
        out_y = [spread, spread]
        if o % 2 == 0:
            out_x[0] = (dx == 0) | (dx == 1)
            out_y[0] = spread | (dy[s] == 1)
        else:
            out_x[1] = (dx == 0) | (dx == 3)
            out_y[1] = spread | (dy[s] == 3)
        return [spread & out_x[0], spread & out_x[1], out_y[0], out_y[1]]

    def row_copy(k, s, o, source):
        return push(
            source, rows.at[s, o], row_sent.at[k, s, o], row_got.at[s, o], sides[k]
        )

    def row_source(o, source=None):
        place = raw.at[zl, block_index(o)] if source is None else source
        for s in (0, 1):

            @pl.when((dx == 0) & (dy[s] == 0))
            def _():
                for k in range(4):
                    row_copy(k, s, o, place).start()
                pltpu.make_async_copy(place, rows.at[s, o], row_got.at[s, o]).start()

    def row_step(s, o, least, most):
        place = rows.at[s, o]

        @pl.when((hops[s] >= least) & (hops[s] <= most))
        def _():
            row_copy(0, s, o, place).wait_recv()
            for k, go in enumerate(sends(s, o)):

                @pl.when(go & (hops[s] > 0))
                def _():
                    row_copy(k, s, o, place).start()

    def steps(o, least, most):
        for s in (0, 1):
            row_step(s, o, least, most)

    def error_copy(k, device_):
        return push(error, error, err_sent.at[k], err_got, device_)

    def error_phase(receive, forward):
        @pl.when(receive)
        def _():
            error_copy(0, twin).wait_recv()

        for k, go, target in forward:

            @pl.when(go)
            def _():
                error_copy(k, target).start()

    base_x = (y == 0) & (zl == 0)
    forward_x = [
        (0, base_x & ((x == 0) | (x == 1)), sides[0]),
        (1, base_x & (x == 0), sides[1]),
    ]
    forward_y = [
        (2, (zl == 0) & ((y == 0) | (y == 1)), sides[2]),
        (3, (zl == 0) & (y == 0), sides[3]),
    ]
    forward_z = [(4, zl == 0, partner)]

    def stat_push(buffer, index, sent, got, k, me, target):
        return push(buffer.at[me], buffer.at[me], sent.at[k], got.at[me], target)

    own = pltpu.make_async_copy(act, slot(z, core), own_sem)
    own.start()
    ring(0, 0, act).start()
    ring(1, 0, act).start()
    share(0, act).start()
    row_source(0, act)

    squares = jnp.zeros((act.shape[0], 128), f32)
    for q in range(4):
        piece = act[:, q * 128 : q * 128 + 128].astype(f32)
        squares = squares + piece * piece
    sums = jnp.sum(squares.T, axis=0, keepdims=True)
    stat_x[x] = jnp.broadcast_to(sums, stat_x.shape[1:])

    def x_target(k):
        return device(rem(x + k, 4), y, z, core)

    def y_target(k):
        return device(x, rem(y + k, 4), z, core)

    for k in (1, 2, 3):
        stat_push(stat_x, x, sx_sent, sx_got, k - 1, x, x_target(k)).start()
    own.wait()
    share_wait(0)
    row_source(1)
    for k in (1, 2, 3):
        stat_push(stat_x, x, sx_sent, sx_got, 0, rem(x + k, 4), twin).wait_recv()
    stat_y[y] = stat_x[0] + stat_x[1] + stat_x[2] + stat_x[3]
    for k in (1, 2, 3):
        stat_push(stat_y, y, sy_sent, sy_got, k - 1, y, y_target(k)).start()

    @pl.when(feat == 0)
    def _():
        error[...] = residue[...]

    steps(0, 0, 1)
    steps(1, 0, 0)

    ring_wait(0, 1)
    ring(0, 1).start()
    share(1).start()
    ring_wait(1, 1)
    ring(1, 1).start()
    share(5).start()

    for k in (1, 2, 3):
        stat_push(stat_y, y, sy_sent, sy_got, 0, rem(y + k, 4), twin).wait_recv()
    stat_z[z] = stat_y[0] + stat_y[1] + stat_y[2] + stat_y[3]
    for k in range(1, 8):
        stat_push(
            stat_z, z, sz_sent, sz_got, k - 1, z, device(x, y, along(k), core)
        ).start()
    error_phase(base_x & (x > 0), forward_x)
    steps(0, 2, 3)
    steps(1, 1, 2)

    ring_wait(0, 2)
    ring(0, 2).start()
    share(2).start()
    row_source(2)
    ring_wait(1, 2)
    ring(1, 2).start()
    share(6).start()
    row_source(4)
    share_wait(1)
    share_wait(5)
    share_wait(2)
    row_source(5)
    share_wait(6)
    row_source(3)

    for k in range(1, 8):
        stat_push(stat_z, z, sz_sent, sz_got, 0, along(k), twin).wait_recv()
    for h in range(4):
        stat_all[core, h] = stat_z[2 * h] + stat_z[2 * h + 1]
    push(stat_all.at[core], stat_all.at[core], st_sent, st_got, twin).start()
    error_phase((zl == 0) & (y > 0), forward_y + forward_z)
    steps(0, 4, 4)
    steps(1, 3, 4)
    push(stat_all.at[core], stat_all.at[1 - core], st_sent, st_got, twin).wait_recv()

    width = act.shape[1]
    tokens = raw.shape[1] * raw.shape[2]
    full_width = width * 32
    pair = (x * 4 + y) * 2

    def stand(row):
        return jnp.broadcast_to(row, (128, row.shape[1])).T

    def scale_blocks(rel):
        for cc in (0, 1):
            o = 2 * rel + cc
            part = core if cc == 0 else 1 - core
            whole = stat_all[part, rem(zh + 4 + offsets[rel], 4)][:1, :]
            factors = stand(1.0 / (whole / full_width + norm_epsilon) / tokens)
            index = block_index(o)
            for n in (0, 1):
                weight = gain[pair + n]
                for q in range(4):
                    at = slice(q * 128, q * 128 + 128)
                    piece = raw[n, index, :, at].astype(f32)
                    scaled[n, o, :, at] = (piece * factors * weight[:, at]).astype(bf16)

    half = 256

    def multiply(rel, s):
        def one(step, carry):
            n = div(step, 2)
            at = pl.ds(pl.multiple_of(rem(step, 2) * half, half), half)
            a = rows[s, 2 * rel : 2 * rel + 2, :, at].reshape(-1, half)
            b = scaled[n, 2 * rel : 2 * rel + 2].reshape(-1, width)
            product = lax.dot_general(
                a, b, (((0,), (0,)), ((), ())), preferred_element_type=f32
            )
            if rel == 0:
                total[s, n, at, :] = product
            else:
                total[s, n, at, :] += product
            return carry

        lax.fori_loop(0, 4, one, 0)

    scale_blocks(0)
    steps(2, 0, 1)

    ring_wait(0, 3)
    ring(0, 3).start()
    share(3).start()
    ring_wait(1, 3)
    share(7).start()
    error_phase(zl > 0, [])
    steps(2, 2, 4)
    steps(3, 0, 1)
    steps(4, 0, 0)
    steps(5, 0, 0)

    ring_wait(0, 4)
    share(4).start()
    row_source(6)
    share_wait(3)
    share_wait(7)
    share_wait(4)
    row_source(7)

    multiply(0, 0)
    multiply(0, 1)
    steps(3, 2, 4)
    scale_blocks(1)
    multiply(1, 0)
    multiply(1, 1)
    steps(4, 1, 4)
    steps(5, 1, 4)

    shift = lax.dot_general(
        error[...].astype(f32),
        factor[...],
        (((0,), (0,)), ((), ())),
        precision=lax.Precision.HIGHEST,
        preferred_element_type=f32,
    )
    updated[...] = weights[...] - shift

    @pl.when(feat == 0)
    def _():
        updated[:, :128] = quantized[...].T

    scale_blocks(2)
    multiply(2, 0)
    multiply(2, 1)
    scale_blocks(3)

    def result_copy(s):
        return push(away.at[s], home.at[s], part_sent.at[s], part_got.at[s], partner)

    for s in (0, 1):
        row_step(s, 6, 0, 4)
        row_step(s, 7, 0, 4)
        multiply(3, s)
        lift = stand(gain[(zh * 4 + 2 * core + s) * 2 + zl])
        start = pl.multiple_of((s * 2 + zl) * width, width)
        for q in range(4):
            at = slice(q * 128, q * 128 + 128)
            away[s, :, at] = (total[s, 1 - zl, :, at] * lift).astype(bf16)
        result_copy(s).start()
        for q in range(4):
            at = slice(q * 128, q * 128 + 128)
            hessian[pl.ds(start, width), at] = total[s, zl, :, at] * lift
    for s in (0, 1):
        result_copy(s).wait_recv()
        start = pl.multiple_of((s * 2 + 1 - zl) * width, width)
        hessian[pl.ds(start, width), :] = home[s].astype(f32)

    for hop in range(4):
        ring(0, hop).wait_send()
    for hop in range(3):
        ring(1, hop).wait_send()
    for index in range(8):
        share(index).wait_send()
    for k in (1, 2, 3):
        stat_push(stat_x, x, sx_sent, sx_got, k - 1, x, x_target(k)).wait_send()
        stat_push(stat_y, y, sy_sent, sy_got, k - 1, y, y_target(k)).wait_send()
    for k in range(1, 8):
        stat_push(stat_z, z, sz_sent, sz_got, k - 1, z, behind).wait_send()
    push(stat_all.at[core], stat_all.at[core], st_sent, st_got, twin).wait_send()
    for k, go, target in forward_x + forward_y + forward_z:

        @pl.when(go)
        def _():
            error_copy(k, target).wait_send()

    for o in range(8):
        for s in (0, 1):
            for k, go in enumerate(sends(s, o)):

                @pl.when(go)
                def _():
                    row_copy(k, s, o, rows.at[s, o]).wait_send()

    for s in (0, 1):
        result_copy(s).wait_send()


def body(activations, norm_gain, weights, inverse_factor, grid_scales):
    width = activations.shape[1]
    panel = inverse_factor.shape[0]
    outs = weights.shape[0]
    in_vmem = pl.BlockSpec(memory_space=pltpu.VMEM)
    quantized, residue = pl.pallas_call(
        panel_kernel,
        out_shape=(
            jax.ShapeDtypeStruct((panel, outs), f32),
            jax.ShapeDtypeStruct((panel, outs), bf16),
        ),
        in_specs=[in_vmem] * 3,
        out_specs=(in_vmem, in_vmem),
        scratch_shapes=[pltpu.VMEM((panel, outs), f32)] * 2,
        name="panel",
    )(weights, inverse_factor, grid_scales.reshape(1, outs))
    dma = pltpu.SemaphoreType.DMA
    block = (width, width)
    return tuple(
        pl.pallas_call(
            main_kernel,
            out_shape=(
                jax.ShapeDtypeStruct((4 * width, width), f32),
                jax.ShapeDtypeStruct(weights.shape, f32),
            ),
            in_specs=[in_vmem] * 6,
            out_specs=(in_vmem, in_vmem),
            scratch_shapes=[
                pltpu.VMEM((2, 8) + block, bf16),
                pltpu.VMEM((2, 8) + block, bf16),
                pltpu.VMEM((2, 8) + block, bf16),
                pltpu.VMEM((2, 2) + block, f32),
                pltpu.VMEM((2,) + block, bf16),
                pltpu.VMEM((2,) + block, bf16),
                pltpu.VMEM((4, 8, width), f32),
                pltpu.VMEM((4, 8, width), f32),
                pltpu.VMEM((8, 8, width), f32),
                pltpu.VMEM((2, 4, 8, width), f32),
                pltpu.VMEM((panel, outs), bf16),
                dma,
                dma((8,)),
                dma((8,)),
                dma((8,)),
                dma((8,)),
                dma((4, 2, 8)),
                dma((2, 8)),
                dma((3,)),
                dma((4,)),
                dma((3,)),
                dma((4,)),
                dma((7,)),
                dma((8,)),
                dma,
                dma,
                dma((5,)),
                dma,
                dma((2,)),
                dma((2,)),
            ],
            compiler_params=pltpu.CompilerParams(
                collective_id=0,
                has_side_effects=True,
                vmem_limit_bytes=56 * 1024 * 1024,
            ),
            name="gram",
        )(
            activations,
            norm_gain.reshape(-1, 1, width),
            weights,
            inverse_factor,
            quantized,
            residue,
        )
    )


def solution(mesh):
    placed = (P("dp", "feat"), P(), P("dp", "feat"), P(None, "feat"), P("dp"))
    return jax.shard_map(
        body,
        mesh=mesh,
        in_specs=placed,
        out_specs=(P("dp", "feat"), P("dp", "feat")),
        check_vma=False,
    )
```

time: 941 us -> 233 us (0.25)
  waiting for transfers between devices: 533 us -> 0 us
  Pallas kernels: 0 us -> 226 us
  other arithmetic: 199 us -> 0 us
  local copies, waits for them, and re-layouts: 97.2 us -> 5.7 us
  blocking collectives: 67.3 us -> 0 us
  matrix products: 18.3 us -> 0 us
  between operations: 13.8 us -> 0.65 us
    psum x1 -> x0, waiting for transfers between devices: 262 us -> none  [spread(): return lax.psum(kept, axis)]
    pallas_call x0 -> x2, Pallas kernels: none -> 226 us  [the longest x1 218 us: body(): pl.pallas_call(main_kernel, out_shape=(jax.ShapeDtypeStruct((4 * width, w...]
    reduce_scatter x1 -> x0, waiting for transfers between devices: 190 us -> none  [body(): lax.psum_scatter((product / token_total).astype(jnp.bfloat16), 'dp', scat...]
    div x128 -> x0, other arithmetic: 176 us -> none  [advance(): scaled_error = (current - dequantized) / pivot_entry]
    all_gather x1 -> x0, waiting for transfers between devices: 81.8 us -> none  [body(): gathered = lax.all_gather(normed, 'feat', axis=1, tiled=True)]
    dynamic_slice x129 -> x0, local copies, waits for them, and re-layouts: 80.1 us -> none  [the longest x128 79.3 us: advance(): lax.dynamic_index_in_dim(diagonal_entries, index, 0, keepdims=False)]
    psum x1 -> x0, blocking collectives: 67.3 us -> none  [body(): row_squares = lax.psum(own_squares, 'feat')]
    dot_general x2 -> x0, matrix products: 18.3 us -> none  [the longest x1 15.8 us: body(): lax.dot_general(gathered, normed, (((0,), (0,)), ((), ())), preferred_ele...]
  transfers between devices with their start and end apart: 3 -> 0, of which waited for: 3 -> 0; matrix products, arithmetic and copies ran while one was open for 33% -> 0% of each run, Pallas kernels for 0% -> 0%
where the time goes in v1:
time: 233 us
  Pallas kernels  226 us (97%)
  local copies, waits for them, and re-layouts  5.7 us (2%)
    pallas_call x1, Pallas kernels, body(): pl.pallas_call(main_kernel, out_shape=(jax.ShapeDtypeStruct((4 * width, w...  218 us
    pallas_call x1, Pallas kernels, body(): pl.pallas_call(panel_kernel, out_shape=(jax.ShapeDtypeStruct((panel, outs...  8.5 us
    unnamed x4, local copies, waits for them, and re-layouts  5.7 us

profile of v1, /device:TPU:60, one launch (start us, length us, event | category | flops | bytes accessed | tf_op | source)
XLA Modules:
  0.0 232.7 jit_solution(4149478732963284186)
XLA Ops:
  0.6 8.5 %panel.1 = (f32[128,512]{1,0:T(8,128)}, bf16[128,512]{1,0:T(8,128)(2,1)}) custom-call(f32[512,512]{1,0:T(8,128)} %weights.3, f32[128,512]{1,0:T(8,128)} %factor.3, f32[1,512]{1,0:T(1,128)} %bitcast.3), custom_call_target="tpu_custom_call" | custom-call | tf_op jit(solution)/shard_map/panel/pallas_call | solution.py:496
  9.1 217.9 %gram.1 = (f32[2048,512]{1,0:T(8,128)}, f32[512,512]{1,0:T(8,128)}) custom-call(bf16[512,512]{1,0:T(8,128)(2,1)} %act.1, f32[32,1,512]{2,1,0:T(1,128)} %bitcast.2, f32[512,512]{1,0:T(8,128)} %weights.3, f32[128,512]{1,0:T(8,128)} %factor.3, f32[128,512]{1,0:T(8,128)} %get-tuple-element.4.quantized, bf16[128,512]{1,0:T(8,128)(2,1)} %get-tuple-element.5.residue), custom_call_target="tpu_custom_call" | custom-call | tf_op jit(solution)/shard_map/gram/pallas_call | solution.py:510
  227.0 0.0 copy-start
  227.0 4.7 %copy.9 = f32[2048,512]{1,0:T(8,128)} copy(f32[2048,512]{1,0:T(8,128)} %get-tuple-element.8) | data formatting | bytes 8388608
  231.8 0.0 copy-done
  231.8 1.0 copy.10
Async XLA Ops:
  227.0 4.7 %copy-start = (f32[512,512]{1,0:T(8,128)S(1)}, f32[512,512]{1,0:T(8,128)}, u32[]{:S(2)}) copy-start(f32[512,512]{1,0:T(8,128)} %get-tuple-element.9) | copy-start | bytes 3145732

commit v2 on v1

--- a/solution.py
+++ b/solution.py
@@ -29,7 +29,7 @@
     return part * total
 
 
-def panel_kernel(weights, factor, grid_scales, quantized, residue, ratios, waves):
+def solve_panel(weights, factor, grid_scales, quantized, residue, ratios, waves):
     panel = factor.shape[0]
     block = factor[:, :panel]
     rows = lax.broadcasted_iota(jnp.int32, (panel, panel), 0)
@@ -75,10 +75,12 @@
     gain,
     weights,
     factor,
-    quantized,
-    residue,
+    grid_scales,
     hessian,
     updated,
+    quantized,
+    ratios,
+    waves,
     raw,
     scaled,
     rows,
@@ -185,10 +187,16 @@
 
     offsets = (0, -sign, sign, 2)
     dx = rem(x + 4 - zh, 4)
-    dy = [rem(y + 4 - (2 * core + s), 4) for s in (0, 1)]
-    hops = [
-        jnp.minimum(dx, 4 - dx) + jnp.minimum(dy[s], 4 - dy[s]) for s in (0, 1)
-    ]
+
+    def turn(s):
+        return rem(y + 4 - (2 * core + s), 4)
+
+    def hops(s):
+        return jnp.minimum(dx, 4 - dx) + jnp.minimum(turn(s), 4 - turn(s))
+
+    near = jnp.where(hops(0) < hops(1), 0, 1)
+    far = 1 - near
+    level = hops(near)
 
     def block_index(o):
         part = core if o % 2 == 0 else 1 - core
@@ -196,15 +204,15 @@
 
     def sends(s, o):
         side_x, side_y = (1, 1) if o % 2 == 0 else (3, 3)
-        spread = dy[s] == 0
+        spread = turn(s) == 0
         out_x = [dx == 0, dx == 0]
         out_y = [spread, spread]
         if o % 2 == 0:
             out_x[0] = (dx == 0) | (dx == 1)
-            out_y[0] = spread | (dy[s] == 1)
+            out_y[0] = spread | (turn(s) == 1)
         else:
             out_x[1] = (dx == 0) | (dx == 3)
-            out_y[1] = spread | (dy[s] == 3)
+            out_y[1] = spread | (turn(s) == 3)
         return [spread & out_x[0], spread & out_x[1], out_y[0], out_y[1]]
 
     def row_copy(k, s, o, source):
@@ -216,27 +224,50 @@
         place = raw.at[zl, block_index(o)] if source is None else source
         for s in (0, 1):
 
-            @pl.when((dx == 0) & (dy[s] == 0))
+            @pl.when((dx == 0) & (turn(s) == 0))
             def _():
                 for k in range(4):
                     row_copy(k, s, o, place).start()
                 pltpu.make_async_copy(place, rows.at[s, o], row_got.at[s, o]).start()
 
-    def row_step(s, o, least, most):
+    def row_step(s, o):
         place = rows.at[s, o]
-
-        @pl.when((hops[s] >= least) & (hops[s] <= most))
-        def _():
-            row_copy(0, s, o, place).wait_recv()
-            for k, go in enumerate(sends(s, o)):
-
-                @pl.when(go & (hops[s] > 0))
+        row_copy(0, s, o, place).wait_recv()
+        for k, go in enumerate(sends(s, o)):
+
+            @pl.when(go & (hops(s) > 0))
+            def _():
+                row_copy(k, s, o, place).start()
+
+    done = [set() for _ in range(4)]
+
+    def steps(pieces):
+        for distance, listed in pieces.items():
+            fresh = [p for p in listed if p not in done[distance]]
+            done[distance].update(fresh)
+            if fresh:
+
+                @pl.when(level == distance)
                 def _():
-                    row_copy(k, s, o, place).start()
-
-    def steps(o, least, most):
-        for s in (0, 1):
-            row_step(s, o, least, most)
+                    for which, o in fresh:
+                        row_step(far if which else near, o)
+
+    def everywhere(*listed):
+        for piece in listed:
+            late = [k for k in range(4) if piece not in done[k]]
+            for k in late:
+                done[k].add(piece)
+            s = far if piece[0] else near
+            if len(late) == 4:
+                row_step(s, piece[1])
+            elif late:
+                test = level == late[0]
+                for k in late[1:]:
+                    test = test | (level == k)
+
+                @pl.when(test)
+                def _():
+                    row_step(s, piece[1])
 
     def error_copy(k, device_):
         return push(error, error, err_sent.at[k], err_got, device_)
@@ -266,28 +297,26 @@
     def stat_push(buffer, index, sent, got, k, me, target):
         return push(buffer.at[me], buffer.at[me], sent.at[k], got.at[me], target)
 
+    def x_target(k):
+        return device(rem(x + k, 4), y, z, core)
+
+    def y_target(k):
+        return device(x, rem(y + k, 4), z, core)
+
     own = pltpu.make_async_copy(act, slot(z, core), own_sem)
     own.start()
-    ring(0, 0, act).start()
-    ring(1, 0, act).start()
-    share(0, act).start()
-    row_source(0, act)
-
     squares = jnp.zeros((act.shape[0], 128), f32)
     for q in range(4):
         piece = act[:, q * 128 : q * 128 + 128].astype(f32)
         squares = squares + piece * piece
     sums = jnp.sum(squares.T, axis=0, keepdims=True)
     stat_x[x] = jnp.broadcast_to(sums, stat_x.shape[1:])
-
-    def x_target(k):
-        return device(rem(x + k, 4), y, z, core)
-
-    def y_target(k):
-        return device(x, rem(y + k, 4), z, core)
-
     for k in (1, 2, 3):
         stat_push(stat_x, x, sx_sent, sx_got, k - 1, x, x_target(k)).start()
+    ring(0, 0, act).start()
+    ring(1, 0, act).start()
+    share(0, act).start()
+    row_source(0, act)
     own.wait()
     share_wait(0)
     row_source(1)
@@ -299,10 +328,14 @@
 
     @pl.when(feat == 0)
     def _():
-        error[...] = residue[...]
-
-    steps(0, 0, 1)
-    steps(1, 0, 0)
+        solve_panel(weights, factor, grid_scales, quantized, error, ratios, waves)
+        for k, go, target in forward_x:
+
+            @pl.when(go)
+            def _():
+                error_copy(k, target).start()
+
+    steps({0: [(1, 0)], 1: [(0, 0)]})
 
     ring_wait(0, 1)
     ring(0, 1).start()
@@ -318,9 +351,13 @@
         stat_push(
             stat_z, z, sz_sent, sz_got, k - 1, z, device(x, y, along(k), core)
         ).start()
-    error_phase(base_x & (x > 0), forward_x)
-    steps(0, 2, 3)
-    steps(1, 1, 2)
+    steps({0: [(1, 1)], 1: [(0, 1), (1, 0)], 2: [(0, 0)]})
+    error_phase(base_x & (x == 1), [(0, base_x & (x == 1), sides[0])])
+    steps({1: [(1, 1)], 2: [(0, 1)]})
+    error_phase(
+        base_x & (x > 1),
+        [(2, base_x, sides[2]), (3, base_x, sides[3])],
+    )
 
     ring_wait(0, 2)
     ring(0, 2).start()
@@ -342,10 +379,9 @@
     for h in range(4):
         stat_all[core, h] = stat_z[2 * h] + stat_z[2 * h + 1]
     push(stat_all.at[core], stat_all.at[core], st_sent, st_got, twin).start()
-    error_phase((zl == 0) & (y > 0), forward_y + forward_z)
-    steps(0, 4, 4)
-    steps(1, 3, 4)
+    steps({2: [(1, 0)], 3: [(0, 0)]})
     push(stat_all.at[core], stat_all.at[1 - core], st_sent, st_got, twin).wait_recv()
+    steps({2: [(1, 1)], 3: [(0, 1), (1, 0)]})
 
     width = act.shape[1]
     tokens = raw.shape[1] * raw.shape[2]
@@ -388,19 +424,39 @@
 
         lax.fori_loop(0, 4, one, 0)
 
-    scale_blocks(0)
-    steps(2, 0, 1)
+    def result_copy(s):
+        return push(away.at[s], home.at[s], part_sent.at[s], part_got.at[s], partner)
+
+    def epilogue(s):
+        lift = stand(gain[(zh * 4 + 2 * core + s) * 2 + zl])
+        start = pl.multiple_of((s * 2 + zl) * width, width)
+        for q in range(4):
+            at = slice(q * 128, q * 128 + 128)
+            away[s, :, at] = (total[s, 1 - zl, :, at] * lift).astype(bf16)
+        result_copy(s).start()
+        for q in range(4):
+            at = slice(q * 128, q * 128 + 128)
+            hessian[pl.ds(start, width), at] = (total[s, zl, :, at] * lift).astype(bf16)
+
+    def finish(s):
+        result_copy(s).wait_recv()
+        start = pl.multiple_of((s * 2 + 1 - zl) * width, width)
+        hessian[pl.ds(start, width), :] = home[s]
+
+    steps({0: [(1, 2)], 1: [(0, 2)]})
 
     ring_wait(0, 3)
     ring(0, 3).start()
     share(3).start()
     ring_wait(1, 3)
     share(7).start()
-    error_phase(zl > 0, [])
-    steps(2, 2, 4)
-    steps(3, 0, 1)
-    steps(4, 0, 0)
-    steps(5, 0, 0)
+    error_phase(
+        (zl == 0) & ((y == 1) | (y == 3)),
+        [(2, (zl == 0) & (y == 1), sides[2]), (4, (zl == 0) & (y != 2), partner)],
+    )
+    steps({0: [(1, 3)], 1: [(0, 3), (1, 2)], 2: [(0, 2)], 3: [(1, 1)]})
+    scale_blocks(0)
+    steps({0: [(1, 4)]})
 
     ring_wait(0, 4)
     share(4).start()
@@ -409,16 +465,31 @@
     share_wait(7)
     share_wait(4)
     row_source(7)
-
-    multiply(0, 0)
-    multiply(0, 1)
-    steps(3, 2, 4)
+    everywhere((0, 0), (0, 1), (1, 0), (1, 1))
+    error_phase((zl == 0) & (y == 2), [(4, (zl == 0) & (y == 2), partner)])
+    multiply(0, near)
+    everywhere((0, 2), (0, 3))
+    multiply(0, far)
+    everywhere((1, 2), (0, 4))
     scale_blocks(1)
-    multiply(1, 0)
-    multiply(1, 1)
-    steps(4, 1, 4)
-    steps(5, 1, 4)
-
+    multiply(1, near)
+    everywhere((1, 3), (0, 5))
+    multiply(1, far)
+    scale_blocks(2)
+    everywhere((1, 4))
+    multiply(2, near)
+    everywhere((0, 6), (1, 5))
+    scale_blocks(3)
+    everywhere((0, 7))
+    multiply(2, far)
+    everywhere((1, 6))
+    multiply(3, near)
+    epilogue(near)
+    everywhere((1, 7))
+    multiply(3, far)
+    epilogue(far)
+
+    error_phase(zl > 0, [])
     shift = lax.dot_general(
         error[...].astype(f32),
         factor[...],
@@ -432,31 +503,8 @@
     def _():
         updated[:, :128] = quantized[...].T
 
-    scale_blocks(2)
-    multiply(2, 0)
-    multiply(2, 1)
-    scale_blocks(3)
-
-    def result_copy(s):
-        return push(away.at[s], home.at[s], part_sent.at[s], part_got.at[s], partner)
-
-    for s in (0, 1):
-        row_step(s, 6, 0, 4)
-        row_step(s, 7, 0, 4)
-        multiply(3, s)
-        lift = stand(gain[(zh * 4 + 2 * core + s) * 2 + zl])
-        start = pl.multiple_of((s * 2 + zl) * width, width)
-        for q in range(4):
-            at = slice(q * 128, q * 128 + 128)
-            away[s, :, at] = (total[s, 1 - zl, :, at] * lift).astype(bf16)
-        result_copy(s).start()
-        for q in range(4):
-            at = slice(q * 128, q * 128 + 128)
-            hessian[pl.ds(start, width), at] = total[s, zl, :, at] * lift
-    for s in (0, 1):
-        result_copy(s).wait_recv()
-        start = pl.multiple_of((s * 2 + 1 - zl) * width, width)
-        hessian[pl.ds(start, width), :] = home[s].astype(f32)
+    finish(near)
+    finish(far)
 
     for hop in range(4):
         ring(0, hop).wait_send()
@@ -493,29 +541,21 @@
     panel = inverse_factor.shape[0]
     outs = weights.shape[0]
     in_vmem = pl.BlockSpec(memory_space=pltpu.VMEM)
-    quantized, residue = pl.pallas_call(
-        panel_kernel,
-        out_shape=(
-            jax.ShapeDtypeStruct((panel, outs), f32),
-            jax.ShapeDtypeStruct((panel, outs), bf16),
-        ),
-        in_specs=[in_vmem] * 3,
-        out_specs=(in_vmem, in_vmem),
-        scratch_shapes=[pltpu.VMEM((panel, outs), f32)] * 2,
-        name="panel",
-    )(weights, inverse_factor, grid_scales.reshape(1, outs))
     dma = pltpu.SemaphoreType.DMA
     block = (width, width)
-    return tuple(
+    hessian, updated = (
         pl.pallas_call(
             main_kernel,
             out_shape=(
-                jax.ShapeDtypeStruct((4 * width, width), f32),
+                jax.ShapeDtypeStruct((4 * width, width), bf16),
                 jax.ShapeDtypeStruct(weights.shape, f32),
             ),
-            in_specs=[in_vmem] * 6,
+            in_specs=[in_vmem] * 5,
             out_specs=(in_vmem, in_vmem),
             scratch_shapes=[
+                pltpu.VMEM((panel, outs), f32),
+                pltpu.VMEM((panel, outs), f32),
+                pltpu.VMEM((panel, outs), f32),
                 pltpu.VMEM((2, 8) + block, bf16),
                 pltpu.VMEM((2, 8) + block, bf16),
                 pltpu.VMEM((2, 8) + block, bf16),
@@ -558,10 +598,10 @@
             norm_gain.reshape(-1, 1, width),
             weights,
             inverse_factor,
-            quantized,
-            residue,
+            grid_scales.reshape(1, outs),
         )
     )
+    return hessian.astype(f32), updated
 
 
 def solution(mesh):

time: 233 us -> 143 us (0.61)
  Pallas kernels: 226 us -> 137 us
  local copies, waits for them, and re-layouts: 5.7 us -> 0.97 us
  other arithmetic: 0 us -> 4.29 us
    pallas_call x1, Pallas kernels: 218 us -> 137 us  [body(): pl.pallas_call(main_kernel, out_shape=(jax.ShapeDtypeStruct((4 * width, w...]
    pallas_call x1 -> x0, Pallas kernels: 8.5 us -> none  [body(): pl.pallas_call(panel_kernel, out_shape=(jax.ShapeDtypeStruct((panel, outs...]
    unnamed x4 -> x3, local copies, waits for them, and re-layouts: 5.7 us -> 0.97 us
    convert_element_type x0 -> x1, other arithmetic: none -> 4.29 us  [body(): return (hessian.astype(f32), updated)]
where the time goes in v2:
time: 143 us
  Pallas kernels  137 us (96%)
  other arithmetic  4.29 us (3%)
    pallas_call x1, Pallas kernels, body(): pl.pallas_call(main_kernel, out_shape=(jax.ShapeDtypeStruct((4 * width, w...  137 us
    convert_element_type x1, other arithmetic, body(): return (hessian.astype(f32), updated)  4.29 us

profile of v2, /device:TPU:60, one launch (start us, length us, event | category | flops | bytes accessed | tf_op | source)
XLA Modules:
  0.0 143.1 jit_solution(13156392075704614672)
XLA Ops:
  0.6 137.2 %gram.1 = (bf16[2048,512]{1,0:T(8,128)(2,1)}, f32[512,512]{1,0:T(8,128)}) custom-call(bf16[512,512]{1,0:T(8,128)(2,1)} %act.1, f32[32,1,512]{2,1,0:T(1,128)} %bitcast.2, f32[512,512]{1,0:T(8,128)} %weights.1, f32[128,512]{1,0:T(8,128)} %factor.1, f32[1,512]{1,0:T(1,128)} %bitcast.3), custom_call_target="tpu_custom_call" | custom-call | tf_op jit(solution)/shard_map/gram/pallas_call | solution.py:547
  137.8 0.0 copy-start
  137.8 4.3 %convert_element_type.3 = f32[2048,512]{1,0:T(8,128)} convert(bf16[2048,512]{1,0:T(8,128)(2,1)} %get-tuple-element.4) | non-fusion elementwise | flops 1048576 | bytes 6291456 | tf_op jit(solution)/shard_map/convert_element_type | solution.py:604
  142.1 0.0 copy-done
  142.1 1.0 copy.8
Async XLA Ops:
  137.8 4.3 %copy-start = (f32[512,512]{1,0:T(8,128)S(1)}, f32[512,512]{1,0:T(8,128)}, u32[]{:S(2)}) copy-start(f32[512,512]{1,0:T(8,128)} %get-tuple-element.9) | copy-start | bytes 3145732
